TPU v7x, 128 devices: a whole 4x4x4 slice. The times are simulated.
128 devices in a mesh: stretch: 4 (over z_lo, core), mp: 32 (over x, y, z_hi).
Axes of the slice: x: 4, y: 4, z: 4 (z_hi: 2, z_lo: 2; z = z_hi * 2 + z_lo), core: 2. Of those that a mesh axis runs over, the one named last changes fastest.
Arguments:
- states: bfloat16 [4, 4096, 3072], P('stretch', 'mp'), may hold values from -6 to 6
- queries: bfloat16 [4, 4096, 1536], P('stretch', 'mp'), may hold values from -32 to 32
- keys: bfloat16 [4, 4096, 512], P('stretch', 'mp'), may hold values from -6 to 6
- values: bfloat16 [4, 4096, 512], P('stretch', 'mp'), may hold values from -6 to 6
- out_weight: bfloat16 [1536, 3072], replicated, may hold values from -0.15625 to 0.15625
- norm_gain: float32 [3072], replicated, may hold values from 0.1 to 1.9
- gate_table: float32 [64, 3072], replicated, may hold values from 0.5 to 1.5
- noise_steps: int32 [4], P('stretch'), may hold values from 0 to 63, as said below
- block_order: int32 [4], replicated, may hold values from 0 to 31, as said below
Outputs:
- mixed: bfloat16 [4, 4096, 3072], P('stretch', 'mp')
Inputs may be any that keep to these rules, and one draw needn't show every extreme that they name: `noise_steps`: the latent blocks are at distinct noise levels. `block_order`: distinct positions; only their order matters.
All inputs are finite; a program needn't handle non-finite values.
Results may differ from a plain program's by a relative error of at most 0.011.
Values may be sent and summed in bfloat16 or wider, within the bound.
A program may use at most 128 MiB of HBM per device.

v0:
```python
import math

import jax
import jax.numpy as jnp
from jax import lax
from jax.sharding import PartitionSpec as P

HEAD_SIZE = 128


def attend_block(carry, query_heads, key_piece, value_piece, valid_rows):
    running, total, accum = carry
    scale = 1.0 / math.sqrt(query_heads.shape[3])
    scores = (
        jnp.einsum("tkgd,nkd->kgtn", query_heads, key_piece, preferred_element_type=jnp.float32)
        * scale
    )
    mask = valid_rows[None, None, None, :]
    scores = jnp.where(mask, scores, -1e30)
    new_top = jnp.maximum(running, jnp.max(scores, axis=3))
    weights = jnp.where(mask, jnp.exp(scores - new_top[..., None]), 0.0)
    fade = jnp.exp(running - new_top)
    total = total * fade + jnp.sum(weights, axis=3)
    summed = jnp.einsum(
        "kgtn,nkd->kgtd",
        weights.astype(jnp.bfloat16),
        value_piece,
        preferred_element_type=jnp.float32,
    )
    accum = accum * fade[..., None] + summed
    return (new_top, total, accum)


def attend_rows(carry, query_heads, key_piece, value_piece, valid_rows):
    count = key_piece.shape[0]
    width = math.gcd(count, 1024)

    def advance(number, state):
        offset = number * width
        return attend_block(
            state,
            query_heads,
            lax.dynamic_slice_in_dim(key_piece, offset, width, 0),
            lax.dynamic_slice_in_dim(value_piece, offset, width, 0),
            lax.dynamic_slice_in_dim(valid_rows, offset, width, 0),
        )

    return lax.fori_loop(0, count // width, advance, carry)


def empty_state(kv_heads, head_groups, rows):
    return (
        jnp.full((kv_heads, head_groups, rows), -1e30, jnp.float32),
        jnp.zeros((kv_heads, head_groups, rows), jnp.float32),
        jnp.zeros((kv_heads, head_groups, rows, HEAD_SIZE), jnp.float32),
    )


def local(
    states, queries, keys, values, out_weight, norm_gain, gate_table, noise_steps, block_order
):
    tokens = queries.shape[1]
    kv_width = keys.shape[2]
    kv_heads = kv_width // HEAD_SIZE
    head_groups = queries.shape[2] // kv_width
    blocks = block_order.shape[0]
    lanes = jnp.arange(blocks, dtype=jnp.int32)
    myself = lax.axis_index("stretch")
    my_place = jnp.sum(jnp.where(lanes == myself, block_order, 0))
    visible = block_order <= my_place
    query_heads = queries[0].reshape(tokens, kv_heads, head_groups, HEAD_SIZE)
    start_state = empty_state(kv_heads, head_groups, tokens)
    near_keys, near_values = (
        lax.all_gather(keys, "stretch", axis=0, tiled=True),
        lax.all_gather(values, "stretch", axis=0, tiled=True),
    )
    key_rows = lax.all_gather(near_keys, "mp", axis=1, tiled=True)
    value_rows = lax.all_gather(near_values, "mp", axis=1, tiled=True)
    count = key_rows.shape[1]
    valid_rows = jnp.repeat(visible, count)
    running, total, accum = attend_rows(
        start_state,
        query_heads,
        key_rows.reshape(blocks * count, kv_heads, HEAD_SIZE),
        value_rows.reshape(blocks * count, kv_heads, HEAD_SIZE),
        valid_rows,
    )
    heads = accum / total[..., None]
    attended = (
        heads.transpose(2, 0, 1, 3)
        .reshape(tokens, kv_heads * head_groups * HEAD_SIZE)
        .astype(jnp.bfloat16)
    )
    projected = jnp.dot(attended, out_weight, preferred_element_type=jnp.float32)
    normed = (
        projected
        * lax.rsqrt(jnp.mean(projected * projected, axis=-1, keepdims=True) + 1e-06)
        * norm_gain
    )
    noise_levels = jnp.arange(gate_table.shape[0], dtype=jnp.int32)
    gate = jnp.sum(jnp.where(noise_levels[:, None] == noise_steps[0], gate_table, 0.0), axis=0)
    mixed = (states[0].astype(jnp.float32) + gate * normed).astype(jnp.bfloat16)
    return mixed[None]


def solution(mesh):
    placed = (
        P("stretch", "mp", None),
        P("stretch", "mp", None),
        P("stretch", "mp", None),
        P("stretch", "mp", None),
        P(),
        P(),
        P(),
        P("stretch"),
        P(),
    )
    return jax.shard_map(
        local, mesh=mesh, in_specs=placed, out_specs=P("stretch", "mp", None), check_vma=False
    )
```

profile of v0, /device:TPU:1, one launch (start us, length us, event | category | flops | bytes accessed | tf_op | source)
XLA Modules:
  0.0 587.8 jit_solution(5208284936269054891)
XLA Ops:
  6.5 10.4 %all_gather.12 = bf16[4,128,512]{2,1,0:T(8,128)(2,1)} all-gather(bf16[1,128,512]{2,1,0:T(8,128)(2,1)} %param.13), channel_id=1, replica_groups=mesh['stretch'=4,'mp'=32] {'stretch'}, dimensions={0}, use_global_device_ids=true | all-gather | bytes 655360 | tf_op jit(solution)/shard_map/all_gather | solution.py:74
  17.0 8.0 %all_gather.14 = bf16[4,128,512]{2,1,0:T(8,128)(2,1)} all-gather(bf16[1,128,512]{2,1,0:T(8,128)(2,1)} %param.14), channel_id=1, replica_groups=mesh['stretch'=4,'mp'=32] {'stretch'}, dimensions={0}, use_global_device_ids=true | all-gather | bytes 655360 | tf_op jit(solution)/shard_map/all_gather | solution.py:75
  31.2 143.9 %all-gather.3.cloned.1.call-done = bf16[4,4096,512]{2,1,0:T(8,128)(2,1)} async-done(((bf16[4,128,512]{2,1,0:T(8,128)(2,1)}), bf16[4,4096,512]{2,1,0:T(8,128)(2,1)}) %all-gather.3.cloned.1.call-update) | async-done | bytes 16777232 | tf_op jit(solution)/shard_map/all_gather | solution.py:77
  175.1 23.9 %reshape.33 = bf16[16384,4,128]{2,1,0:T(4,128)(2,1)} reshape(bf16[4,4096,512]{2,1,0:T(8,128)(2,1)} %all-gather.3.cloned.1.call-done) | data formatting | bytes 33554432 | tf_op jit(solution)/shard_map/reshape | solution.py:84
  199.0 133.8 %all-gather.5.cloned.1.call-done = bf16[4,4096,512]{2,1,0:T(8,128)(2,1)} async-done(((bf16[4,128,512]{2,1,0:T(8,128)(2,1)}), bf16[4,4096,512]{2,1,0:T(8,128)(2,1)}) %all-gather.5.cloned.1.call-update) | async-done | bytes 16777232 | tf_op jit(solution)/shard_map/all_gather | solution.py:78
  332.8 23.7 %reshape.34 = bf16[16384,4,128]{2,1,0:T(4,128)(2,1)} reshape(bf16[4,4096,512]{2,1,0:T(8,128)(2,1)} %all-gather.5.cloned.1.call-done) | data formatting | bytes 33554432 | tf_op jit(solution)/shard_map/reshape | solution.py:85
  356.6 217.5 %while.18 = (s32[]{:T(128)}, f32[4,3,128]{2,1,0:T(4,128)S(1)}, f32[4,3,128]{2,1,0:T(4,128)S(1)}, f32[4,3,128,128]{3,2,1,0:T(8,128)S(1)}, pred[16384]{0:T(1024)(1...) while((s32[]{:T(128)}, f32[4,3,128]{2,1,0:T(4,128)S(1)}, ...), condition=%wide.region_5.6_spmd.clone, body=%wide.region_2.5_spmd.clone.sunk | while | flops 826351104 | bytes 52401360 | solution.py:48
  358.9 3.9 bitcast_reduce_fusion.2
  362.7 3.9 fusion.29
  367.4 2.8 fusion.31
  372.4 3.9 bitcast_reduce_fusion.2
  376.3 3.9 fusion.29
  381.0 2.8 fusion.31
  386.0 3.9 bitcast_reduce_fusion.2
  389.9 3.9 fusion.29
  394.6 2.8 fusion.31
  399.6 3.9 bitcast_reduce_fusion.2
  403.5 3.9 fusion.29
  413.2 3.9 bitcast_reduce_fusion.2
  417.1 3.9 fusion.29
  421.8 2.8 fusion.31
  426.8 3.9 bitcast_reduce_fusion.2
  430.7 3.9 fusion.29
  440.4 3.9 bitcast_reduce_fusion.2
  444.3 3.9 fusion.29
  448.9 2.8 fusion.31
  454.0 3.9 bitcast_reduce_fusion.2
  457.9 3.9 fusion.29
  467.6 3.9 bitcast_reduce_fusion.2
  471.5 3.9 fusion.29
  476.1 2.8 fusion.31
  481.2 3.9 bitcast_reduce_fusion.2
  485.1 3.9 fusion.29
  494.8 3.9 bitcast_reduce_fusion.2
  498.7 3.9 fusion.29
  503.3 2.8 fusion.31
  508.4 3.9 bitcast_reduce_fusion.2
  512.3 3.9 fusion.29
  522.0 3.9 bitcast_reduce_fusion.2
  525.9 3.9 fusion.29
  530.5 2.8 fusion.31
  535.6 3.9 bitcast_reduce_fusion.2
  539.5 3.9 fusion.29
  549.2 3.9 bitcast_reduce_fusion.2
  553.1 3.9 fusion.29
  562.8 3.9 bitcast_reduce_fusion.2
  566.7 3.9 fusion.29
  574.5 5.2 multiply_reduce_fusion
  (143 shorter events, 77.3 us)
Async XLA Ops:
  6.5 168.6 %all-gather.3.cloned.1.call-start = ((), (), s32[]{:S(2)}) async-start(), calls=%async_computation | async-start | bytes 17301504 | tf_op jit(solution)/shard_map/all_gather | solution.py:77
  17.0 315.9 %all-gather.5.cloned.1.call-start = ((), (), s32[]{:S(2)}) async-start(), calls=%async_computation.1 | async-start | bytes 17301504 | tf_op jit(solution)/shard_map/all_gather | solution.py:78
  362.7 4.6 copy-start
  376.3 4.6 copy-start
  389.9 4.6 copy-start
  403.5 4.6 copy-start
  417.1 4.6 copy-start
  430.7 4.6 copy-start
  444.3 4.6 copy-start
  457.9 4.6 copy-start
  471.5 4.6 copy-start
  485.1 4.6 copy-start
  498.7 4.6 copy-start
  512.3 4.6 copy-start
  525.9 4.6 copy-start
  539.5 4.6 copy-start
  553.1 4.6 copy-start
  566.7 4.6 copy-start
  574.4 5.3 copy-start.1
  574.5 5.3 copy-start.2
Sparse Core Ops, SparseCore 0:
  17.1 157.9 all-gather.2
  178.2 154.5 all-gather.4
where the time goes:
time: 590 us; the launch traced here: 588 us
  waiting for transfers between devices  278 us (47%)
  matrix products  111 us (19%)
  local copies, waits for them, and re-layouts  97.1 us (16%)
  other arithmetic  68.2 us (12%)
  blocking collectives  18.4 us (3%)
  between operations  14.2 us (2%)
    all_gather x1, waiting for transfers between devices, local(): key_rows = lax.all_gather(near_keys, 'mp', axis=1, tiled=True)  144 us
    all_gather x1, waiting for transfers between devices, local(): value_rows = lax.all_gather(near_values, 'mp', axis=1, tiled=True)  134 us
    reduce_sum x16, other arithmetic, attend_block(): total = total * fade + jnp.sum(weights, axis=3)  62.5 us
    dot_general x16, matrix products, attend_block(): jnp.einsum('tkgd,nkd->kgtn', query_heads, key_piece, preferred_element_ty...  62 us
    dot_general x16, matrix products, attend_block(): jnp.einsum('kgtn,nkd->kgtd', weights.astype(jnp.bfloat16), value_piece, p...  44.1 us
    dynamic_slice x16, local copies, waits for them, and re-layouts, advance(): lax.dynamic_slice_in_dim(value_piece, offset, width, 0)  36.3 us
    reshape x1, local copies, waits for them, and re-layouts, local(): key_rows.reshape(blocks * count, kv_heads, HEAD_SIZE)  23.9 us
    reshape x1, local copies, waits for them, and re-layouts, local(): value_rows.reshape(blocks * count, kv_heads, HEAD_SIZE)  23.7 us
  transfers between devices with their start and end apart: 2, of which 2 were waited for; matrix products, arithmetic and copies ran while one was open for 5% of the time, Pallas kernels for 0%

commit v1 on v0

v1 whole, which is shorter than its diff:
```python
import functools
import math

import jax
import jax.numpy as jnp
from jax import lax
from jax.experimental import pallas as pl
from jax.experimental.pallas import tpu as pltpu
from jax.sharding import PartitionSpec as P

HEAD = 128
KV_HEADS = 4
GROUP = 3
WIDE = GROUP * HEAD
TOKENS = 128
BLOCKS = 4
D = 3072
QROWS = BLOCKS * WIDE
SCALE = math.log2(math.e) / math.sqrt(HEAD)
MESH = pl.DeviceIdType.MESH
NT = (((1,), (1,)), ((), ()))

STEPS = (
    ("o00", "s00", "o10", "o20"),
    ("s10", "s20", "o01", "o02"),
    ("s01", "s02", "o30", "o11"),
    ("s30", "s11", "o12", "o21"),
    ("s12", "s21", "o22", "o03"),
    ("s22", "s03", "o13", "o23"),
    ("s13", "s23", "o31", "o32"),
    ("s31", "s32", "o33", "s33"),
)
PLACE = {name: i for i, name in enumerate(n for step in STEPS for n in step)}
HALVES = 4
STEP_ROWS = HALVES * TOKENS


def unit_number(name):
    return int(name[1]) * 4 + int(name[2])


def kernel(
    order_ref, noise_ref, q_hbm, k_hbm, v_hbm, states_hbm, w_hbm, gain_ref, gate_hbm,
    out_ref,
    q_in, k_in, v_in, q_two, kv, scores, top, accum, o_out, o_in, w_v, states_v, gate_v, proj,
    qkv_send, qkv_recv, own_recv, sib_recv, own_send, sib_send, o_send, o_recv, fetch_sem,
):
    st = lax.axis_index("stretch")
    mp = lax.axis_index("mp")
    core = lax.rem(st, 2)
    z_hi = lax.rem(mp, 2)
    z = z_hi * 2 + lax.div(st, 2)
    y = lax.rem(lax.div(mp, 2), 4)
    x = lax.div(mp, 8)

    def device(xx, yy, zz, cc):
        return (lax.rem(zz, 2) * 2 + cc, xx * 8 + yy * 2 + lax.div(zz, 2))

    def ring(axis_is_x, by):
        return device(
            lax.rem(x + by * axis_is_x, 4), lax.rem(y + by * (1 - axis_is_x), 4), z, core
        )

    first_is_x = 1 - core
    first_plus, first_minus = ring(first_is_x, 1), ring(first_is_x, 3)
    second_plus, second_minus = ring(core, 1), ring(core, 3)
    sibling = device(x, y, z, 1 - core)

    barrier = pltpu.get_barrier_semaphore()
    for by in range(1, 8):
        other = lax.rem(z * 2 + core + by, 8)
        pl.semaphore_signal(
            barrier, inc=1, device_id=device(x, y, lax.div(other, 2), lax.rem(other, 2)),
            device_id_type=MESH,
        )
    for neighbour in (first_plus, first_minus, second_plus, second_minus):
        pl.semaphore_signal(barrier, inc=1, device_id=neighbour, device_id_type=MESH)
    pl.semaphore_wait(barrier, 11)

    def spread(by, what, near=False):
        h = lax.rem(z + by, 4)
        source, target, width = ((k_hbm, k_in, HEAD), (v_hbm, v_in, HEAD), (q_hbm, q_in, WIDE))[what]
        src = source.at[0, :, pl.ds(pl.multiple_of(h * width, width), width)]
        if near:
            return pltpu.make_async_copy(src, target.at[st], qkv_recv.at[what, st])
        return pltpu.make_async_remote_copy(
            src_ref=src, dst_ref=target.at[st], send_sem=qkv_send.at[what, by],
            recv_sem=qkv_recv.at[what, st], device_id=device(x, y, h, z_hi), device_id_type=MESH,
        )

    stays = core == z_hi
    for what in range(3):
        for by in (2, 1, 3):
            spread(by, what).start()

        @pl.when(stays)
        def _(what=what):
            spread(0, what, True).start()

        @pl.when(jnp.logical_not(stays))
        def _(what=what):
            spread(0, what).start()

    fetches = [
        pltpu.make_async_copy(w_hbm, w_v, fetch_sem.at[0]),
        pltpu.make_async_copy(gate_hbm, gate_v, fetch_sem.at[1]),
        pltpu.make_async_copy(states_hbm, states_v, fetch_sem.at[2]),
    ]
    for fetch in fetches:
        fetch.start()

    def rank_of(b):
        rank, place = jnp.int32(0), order_ref[b]
        for c in range(BLOCKS):
            other = order_ref[c]
            before = (other < place) | ((other == place) & (c < b))
            rank = rank + jnp.where(before, 1, 0)
        return rank

    ranks = [rank_of(jnp.int32(b)) for b in range(BLOCKS)]
    placed = []
    for i in range(BLOCKS):
        at = jnp.int32(0)
        for b in range(BLOCKS):
            at = at + jnp.where(ranks[b] == i, b, 0)
        placed.append(at)

    def landed(what):
        target = (k_in, v_in, q_in)[what]
        for b in range(BLOCKS):
            pltpu.make_async_copy(target.at[b], target.at[b], qkv_recv.at[what, b]).wait()

    def unit(name):
        return kv.at[PLACE[name]]

    def send(number, source, target, sem, to, part=None):
        src, dst = unit(source), unit(target)
        if part is not None:
            src, dst = src.at[part], dst.at[part]
        return pltpu.make_async_remote_copy(
            src_ref=src, dst_ref=dst, send_sem=own_send.at[number], recv_sem=sem,
            device_id=to, device_id_type=MESH,
        )

    def recv_sem(name, part=0):
        return own_recv.at[unit_number(name), part]

    def first_copies():
        return [
            send(0, "o00", "o10", recv_sem("o10"), first_plus),
            send(1, "o00", "o20", recv_sem("o20"), first_minus),
        ]

    def first_forward(side):
        if side == 1:
            return send(2, "o10", "o30", recv_sem("o30", 0), first_plus, 0)
        return send(3, "o20", "o30", recv_sem("o30", 1), first_minus, 1)

    def second_copies(p):
        here = "o%d0" % p
        return [
            send(4 + p * 4, here, "o%d1" % p, recv_sem("o%d1" % p), second_plus),
            send(5 + p * 4, here, "o%d2" % p, recv_sem("o%d2" % p), second_minus),
        ]

    def second_forward(p, side):
        far = "o%d3" % p
        if side == 1:
            return send(6 + p * 4, "o%d1" % p, far, recv_sem(far, 0), second_plus, 0)
        return send(7 + p * 4, "o%d2" % p, far, recv_sem(far, 1), second_minus, 1)

    def share(name):
        number = unit_number(name)
        return pltpu.make_async_remote_copy(
            src_ref=unit(name), dst_ref=unit("s" + name[1:]), send_sem=sib_send.at[number],
            recv_sem=sib_recv.at[number], device_id=sibling, device_id_type=MESH,
        )

    def arrived(name):
        if name[0] == "s":
            pltpu.make_async_copy(unit(name), unit(name), sib_recv.at[unit_number(name)]).wait()
        elif name[1:] == "00":
            pass
        elif "3" in (name[2],) or name[1:] == "30":
            for part in range(2):
                here = unit(name).at[part]
                pltpu.make_async_copy(here, here, recv_sem(name, part)).wait()
        else:
            pltpu.make_async_copy(unit(name), unit(name), recv_sem(name)).wait()

    def take(name):
        arrived(name)
        if name[0] == "s" or name == "o00":
            return
        share(name).start()
        p, s = int(name[1]), int(name[2])
        if s == 0:
            if p in (1, 2):
                first_forward(p).start()
            for copy in second_copies(p):
                copy.start()
        elif s in (1, 2):
            second_forward(p, s).start()

    landed(0)
    landed(1)
    mine = PLACE["o00"]
    for i in range(BLOCKS):
        kv[mine, 0, i] = k_in[placed[i]]
        kv[mine, 1, i] = v_in[placed[i]]
    for copy in first_copies():
        copy.start()
    share("o00").start()
    for copy in second_copies(0):
        copy.start()

    landed(2)
    for i in range(BLOCKS):
        rows = q_in[placed[i]].astype(jnp.float32) * SCALE
        high = rows.astype(jnp.bfloat16)
        low = (rows - high.astype(jnp.float32)).astype(jnp.bfloat16)
        for g in range(GROUP):
            at = i * WIDE + g * HEAD
            q_two[at:at + TOKENS, 0:HEAD] = high[:, g * HEAD:(g + 1) * HEAD]
            q_two[at:at + TOKENS, HEAD:2 * HEAD] = low[:, g * HEAD:(g + 1) * HEAD]

    accum[...] = jnp.zeros_like(accum)
    top[...] = jnp.full_like(top, -1e30)

    def step(g, carry):
        for number, names in enumerate(STEPS):
            @pl.when(g == number)
            def _(names=names):
                for name in names:
                    if name[0] == "o":
                        take(name)
                for name in names:
                    if name[0] == "s":
                        take(name)

        for j in range(BLOCKS):
            keys = jnp.concatenate([kv[g * HALVES + c, 0, j] for c in range(HALVES)], axis=0)
            scores[j, j * WIDE:QROWS] = lax.dot_general(
                q_two[j * WIDE:QROWS], jnp.concatenate([keys, keys], axis=1), NT,
                preferred_element_type=jnp.float32,
            )
        for i in range(BLOCKS):
            rows = slice(i * WIDE, (i + 1) * WIDE)
            old = top[rows]
            most = old
            for j in range(i + 1):
                for t in range(HALVES):
                    most = jnp.maximum(most, scores[j, rows, t * HEAD:(t + 1) * HEAD])
            new = jnp.broadcast_to(jnp.max(most, axis=1, keepdims=True), old.shape)
            top[rows] = new
            fade = jnp.exp2(old - new)
            total = accum[i] * jnp.concatenate([fade, fade], axis=1)
            shift = jnp.concatenate([new] * HALVES, axis=1)
            for j in range(i + 1):
                weights = jnp.exp2(scores[j, rows] - shift).astype(jnp.bfloat16)
                vals = jnp.concatenate([kv[g * HALVES + c, 1, j] for c in range(HALVES)], axis=0)
                vals = jnp.concatenate([vals, jnp.ones_like(vals)], axis=1)
                total = total + jnp.dot(weights, vals, preferred_element_type=jnp.float32)
            accum[i] = total
        return carry

    lax.fori_loop(0, len(STEPS), step, 0)

    def give(by, near=False):
        b = lax.rem(st + by, 4)
        to = device(x, y, core * 2 + lax.div(b, 2), lax.rem(b, 2))
        if near:
            return pltpu.make_async_copy(o_out.at[by], o_in.at[z], o_recv.at[z])
        return pltpu.make_async_remote_copy(
            src_ref=o_out.at[by], dst_ref=o_in.at[z], send_sem=o_send.at[by],
            recv_sem=o_recv.at[z], device_id=to, device_id_type=MESH,
        )

    for by in (2, 1, 3, 0):
        b = lax.rem(st + by, 4)
        block = accum[rank_of(b)]
        heads = (block[:, :HEAD] / block[:, HEAD:]).astype(jnp.bfloat16)
        for g in range(GROUP):
            o_out[by, :, g * HEAD:(g + 1) * HEAD] = heads[g * TOKENS:(g + 1) * TOKENS]
        if by == 0:
            @pl.when(stays)
            def _():
                give(0, True).start()

            @pl.when(jnp.logical_not(stays))
            def _():
                give(0).start()
        else:
            give(by).start()

    for fetch in fetches:
        fetch.wait()
    for h in range(KV_HEADS):
        pltpu.make_async_copy(o_in.at[h], o_in.at[h], o_recv.at[h]).wait()
    attended = jnp.concatenate([o_in[h] for h in range(KV_HEADS)], axis=1)
    squares = jnp.zeros((TOKENS, 1), jnp.float32)
    tile = 512
    for n in range(D // tile):
        part = jnp.dot(
            attended, w_v[:, n * tile:(n + 1) * tile], preferred_element_type=jnp.float32
        )
        proj[:, n * tile:(n + 1) * tile] = part
        squares = squares + jnp.sum(part * part, axis=1, keepdims=True)
    inverse = lax.rsqrt(squares * (1.0 / D) + 1e-06)
    gate = gate_v[pl.ds(noise_ref[0], 1), :] * gain_ref[...]
    out_ref[0] = (
        states_v[0].astype(jnp.float32) + proj[...] * inverse * gate
    ).astype(jnp.bfloat16)

    for what in range(3):
        for by in (1, 2, 3):
            spread(by, what).wait_send()

        @pl.when(jnp.logical_not(stays))
        def _(what=what):
            spread(0, what).wait_send()
    for copy in first_copies() + [first_forward(1), first_forward(2)]:
        copy.wait_send()
    for p in range(4):
        for copy in second_copies(p) + [second_forward(p, 1), second_forward(p, 2)]:
            copy.wait_send()
        for s in range(4):
            share("o%d%d" % (p, s)).wait_send()
    for by in (1, 2, 3):
        give(by).wait_send()

    @pl.when(jnp.logical_not(stays))
    def _():
        give(0).wait_send()


def local(
    states, queries, keys, values, out_weight, norm_gain, gate_table, noise_steps, block_order
):
    hbm = pl.BlockSpec(memory_space=pl.ANY)
    smem = pl.BlockSpec(memory_space=pltpu.SMEM)
    vmem = pl.BlockSpec(memory_space=pltpu.VMEM)
    bf16, f32 = jnp.bfloat16, jnp.float32
    dma = pltpu.SemaphoreType.DMA
    return pl.pallas_call(
        kernel,
        out_shape=jax.ShapeDtypeStruct((1, TOKENS, D), bf16),
        in_specs=[smem, smem, hbm, hbm, hbm, hbm, hbm, vmem, hbm],
        out_specs=vmem,
        scratch_shapes=[
            pltpu.VMEM((BLOCKS, TOKENS, WIDE), bf16),
            pltpu.VMEM((BLOCKS, TOKENS, HEAD), bf16),
            pltpu.VMEM((BLOCKS, TOKENS, HEAD), bf16),
            pltpu.VMEM((QROWS, 2 * HEAD), bf16),
            pltpu.VMEM((32, 2, BLOCKS, TOKENS, HEAD), bf16),
            pltpu.VMEM((BLOCKS, QROWS, STEP_ROWS), f32),
            pltpu.VMEM((QROWS, HEAD), f32),
            pltpu.VMEM((BLOCKS, WIDE, 2 * HEAD), f32),
            pltpu.VMEM((BLOCKS, TOKENS, WIDE), bf16),
            pltpu.VMEM((KV_HEADS, TOKENS, WIDE), bf16),
            pltpu.VMEM((KV_HEADS * WIDE, D), bf16),
            pltpu.VMEM((1, TOKENS, D), bf16),
            pltpu.VMEM(gate_table.shape, f32),
            pltpu.VMEM((TOKENS, D), f32),
            dma((3, 4)), dma((3, 4)), dma((16, 2)), dma((16,)), dma((20,)), dma((16,)),
            dma((4,)), dma((4,)), dma((3,)),
        ],
        compiler_params=pltpu.CompilerParams(
            collective_id=0, has_side_effects=True, vmem_limit_bytes=56 * 2**20
        ),
        cost_estimate=pl.CostEstimate(
            flops=9_300_000_000, bytes_accessed=20_000_000, transcendentals=16_000_000
        ),
        name="attend",
    )(
        block_order, noise_steps, queries, keys, values, states, out_weight,
        norm_gain.reshape(1, D), gate_table,
    )


def solution(mesh):
    placed = (
        P("stretch", "mp", None),
        P("stretch", "mp", None),
        P("stretch", "mp", None),
        P("stretch", "mp", None),
        P(),
        P(),
        P(),
        P("stretch"),
        P(),
    )
    return jax.shard_map(
        local, mesh=mesh, in_specs=placed, out_specs=P("stretch", "mp", None), check_vma=False
    )
```

time: 590 us -> 61.9 us (0.10)
  waiting for transfers between devices: 278 us -> 0 us
  matrix products: 111 us -> 0 us
  local copies, waits for them, and re-layouts: 97.1 us -> 2.06 us
  other arithmetic: 68.2 us -> 0 us
  Pallas kernels: 0 us -> 59 us
  blocking collectives: 18.4 us -> 0 us
  between operations: 14.2 us -> 0.66 us
    all_gather x2 -> x0, waiting for transfers between devices: 278 us -> none  [the longest x1 144 us: local(): key_rows = lax.all_gather(near_keys, 'mp', axis=1, tiled=True)]
    dot_general x33 -> x0, matrix products: 111 us -> none  [the longest x16 62 us: attend_block(): jnp.einsum('tkgd,nkd->kgtn', query_heads, key_piece, preferred_element_ty...]
    reduce_sum x18 -> x0, other arithmetic: 65.1 us -> none  [the longest x16 62.5 us: attend_block(): total = total * fade + jnp.sum(weights, axis=3)]
    pallas_call x0 -> x1, Pallas kernels: none -> 59 us  [local(): pl.pallas_call(kernel, out_shape=jax.ShapeDtypeStruct((1, TOKENS, D), bf1...]
    reshape x2 -> x0, local copies, waits for them, and re-layouts: 47.6 us -> none  [the longest x1 23.9 us: local(): key_rows.reshape(blocks * count, kv_heads, HEAD_SIZE)]
    dynamic_slice x32 -> x0, local copies, waits for them, and re-layouts: 36.4 us -> none  [the longest x16 36.3 us: advance(): lax.dynamic_slice_in_dim(value_piece, offset, width, 0)]
    all_gather x2 -> x0, blocking collectives: 18.4 us -> none  [the longest x1 10.4 us: local(): lax.all_gather(keys, 'stretch', axis=0, tiled=True)]
    while x49 -> x0, local copies, waits for them, and re-layouts: 11.4 us -> none
  transfers between devices with their start and end apart: 2 -> 0, of which waited for: 2 -> 0; matrix products, arithmetic and copies ran while one was open for 5% -> 0% of each run, Pallas kernels for 0% -> 0%
where the time goes in v1:
time: 61.9 us; the launch traced here: 61.7 us
  Pallas kernels  59 us (95%)
  local copies, waits for them, and re-layouts  2.06 us (3%)
  between operations  0.66 us (1%)
    pallas_call x1, Pallas kernels, local(): pl.pallas_call(kernel, out_shape=jax.ShapeDtypeStruct((1, TOKENS, D), bf1...  59 us
    unnamed x1, local copies, waits for them, and re-layouts  2.06 us

profile of v1, /device:TPU:1, one launch (start us, length us, event | category | flops | bytes accessed | tf_op | source)
XLA Modules:
  0.0 61.7 jit_solution(3847496793112215771)
XLA Ops:
  0.7 59.0 %attend.1 = bf16[1,128,3072]{2,1,0:T(8,128)(2,1)} custom-call(s32[4]{0:T(128)} %order_ref.1, s32[1]{0:T(128)S(6)} %copy.11.noise_ref, bf16[1,128,1536]{2,1,0:T(8,128)(2,1)} %q_hbm.1, bf16[1,128,512]{2,1,0:T(8,128)(2,1)} %k_hbm.1, bf16[1,128,512]{2,1,0:T(8,128)(2,1)} %v_hbm.1, bf16[1,128,3072]{2,1,0:T(8,128)(2,1)} %states_hbm.1, bf16[1536,3072]{1,0:T(8,128)(2,1)} %w_hbm.1, ...), custom_call_target="tpu_custom_call" | custom-call | flops 9299999744 | bytes 20000000 | tf_op jit(solution)/shard_map/attend/pallas_call | solution.py:345
  59.6 2.1 %copy.12 = bf16[1,128,3072]{2,1,0:T(8,128)(2,1)} copy(bf16[1,128,3072]{2,1,0:T(8,128)(2,1)} %attend.1) | data formatting | bytes 1572864

commit v2 on v1

--- a/solution.py
+++ b/solution.py
@@ -21,22 +21,69 @@
 NT = (((1,), (1,)), ((), ()))
 
 STEPS = (
-    ("o00", "s00", "o10", "o20"),
-    ("s10", "s20", "o01", "o02"),
-    ("s01", "s02", "o30", "o11"),
-    ("s30", "s11", "o12", "o21"),
-    ("s12", "s21", "o22", "o03"),
-    ("s22", "s03", "o13", "o23"),
-    ("s13", "s23", "o31", "o32"),
-    ("s31", "s32", "o33", "s33"),
+    ("o00", "o20"),
+    ("s00", "s10"),
+    ("s20", "o10"),
+    ("o02", "o01"),
+    ("o12", "o11"),
+    ("o30", "s01"),
+    ("s11", "s02"),
+    ("o22", "s12"),
+    ("o21", "o03"),
+    ("s30", "s21"),
+    ("o32", "s22"),
+    ("o31", "s03"),
+    ("s31", "o13"),
+    ("o23", "o33"),
+    ("s32", "s23"),
+    ("s33", "s13"),
 )
+SENDS = {
+    0: ("S00", "S01"),
+    1: ("S11", "S10"),
+    2: ("f3",),
+    3: ("S20", "S21"),
+    4: ("F0",),
+    6: ("S31", "S30"),
+    7: ("F2",),
+    8: ("o03", "F1"),
+    10: ("F3",),
+    12: ("o23",),
+    14: ("o33",),
+}
 PLACE = {name: i for i, name in enumerate(n for step in STEPS for n in step)}
-HALVES = 4
+HALVES = 2
 STEP_ROWS = HALVES * TOKENS
+FETCH_STEP = 5
 
 
 def unit_number(name):
     return int(name[1]) * 4 + int(name[2])
+
+
+def needed(op):
+    if op == "f3":
+        return ("o10", "o20")
+    if op[0] == "S":
+        return ("o%s0" % op[1],)
+    if op[0] == "F":
+        return ("o%s1" % op[1], "o%s2" % op[1])
+    return (op,)
+
+
+def plan():
+    taken, steps = {"o00"}, []
+    for number, names in enumerate(STEPS):
+        todo = []
+        for op in SENDS.get(number, ()) + names:
+            for name in needed(op):
+                if name not in taken:
+                    taken.add(name)
+                    todo.append(name)
+            if op[0] in "fSF":
+                todo.append(op)
+        steps.append(tuple(todo))
+    return steps
 
 
 def kernel(
@@ -106,9 +153,6 @@
         pltpu.make_async_copy(gate_hbm, gate_v, fetch_sem.at[1]),
         pltpu.make_async_copy(states_hbm, states_v, fetch_sem.at[2]),
     ]
-    for fetch in fetches:
-        fetch.start()
-
     def rank_of(b):
         rank, place = jnp.int32(0), order_ref[b]
         for c in range(BLOCKS):
@@ -145,29 +189,32 @@
     def recv_sem(name, part=0):
         return own_recv.at[unit_number(name), part]
 
-    def first_copies():
+    def first_copies(part):
         return [
-            send(0, "o00", "o10", recv_sem("o10"), first_plus),
-            send(1, "o00", "o20", recv_sem("o20"), first_minus),
+            send(part * 2, "o00", "o10", recv_sem("o10", part), first_plus, part),
+            send(part * 2 + 1, "o00", "o20", recv_sem("o20", part), first_minus, part),
         ]
 
-    def first_forward(side):
-        if side == 1:
-            return send(2, "o10", "o30", recv_sem("o30", 0), first_plus, 0)
-        return send(3, "o20", "o30", recv_sem("o30", 1), first_minus, 1)
-
-    def second_copies(p):
-        here = "o%d0" % p
+    def first_forwards():
         return [
-            send(4 + p * 4, here, "o%d1" % p, recv_sem("o%d1" % p), second_plus),
-            send(5 + p * 4, here, "o%d2" % p, recv_sem("o%d2" % p), second_minus),
+            send(4, "o10", "o30", recv_sem("o30", 0), first_plus, 0),
+            send(5, "o20", "o30", recv_sem("o30", 1), first_minus, 1),
         ]
 
-    def second_forward(p, side):
-        far = "o%d3" % p
-        if side == 1:
-            return send(6 + p * 4, "o%d1" % p, far, recv_sem(far, 0), second_plus, 0)
-        return send(7 + p * 4, "o%d2" % p, far, recv_sem(far, 1), second_minus, 1)
+    def second_copies(p, part):
+        here, at = "o%d0" % p, 6 + p * 6 + part * 2
+        plus, minus = "o%d1" % p, "o%d2" % p
+        return [
+            send(at, here, plus, recv_sem(plus, part), second_plus, part),
+            send(at + 1, here, minus, recv_sem(minus, part), second_minus, part),
+        ]
+
+    def second_forwards(p):
+        far, at = "o%d3" % p, 10 + p * 6
+        return [
+            send(at, "o%d1" % p, far, recv_sem(far, 0), second_plus, 0),
+            send(at + 1, "o%d2" % p, far, recv_sem(far, 1), second_minus, 1),
+        ]
 
     def share(name):
         number = unit_number(name)
@@ -176,43 +223,32 @@
             recv_sem=sib_recv.at[number], device_id=sibling, device_id_type=MESH,
         )
 
-    def arrived(name):
-        if name[0] == "s":
-            pltpu.make_async_copy(unit(name), unit(name), sib_recv.at[unit_number(name)]).wait()
-        elif name[1:] == "00":
-            pass
-        elif "3" in (name[2],) or name[1:] == "30":
+    def begin(copies):
+        for copy in copies:
+            copy.start()
+
+    def act(op):
+        if op == "f3":
+            begin(first_forwards())
+        elif op[0] == "S":
+            begin(second_copies(int(op[1]), int(op[2])))
+        elif op[0] == "F":
+            begin(second_forwards(int(op[1])))
+        elif op[0] == "s":
+            pltpu.make_async_copy(unit(op), unit(op), sib_recv.at[unit_number(op)]).wait()
+        else:
             for part in range(2):
-                here = unit(name).at[part]
-                pltpu.make_async_copy(here, here, recv_sem(name, part)).wait()
-        else:
-            pltpu.make_async_copy(unit(name), unit(name), recv_sem(name)).wait()
-
-    def take(name):
-        arrived(name)
-        if name[0] == "s" or name == "o00":
-            return
-        share(name).start()
-        p, s = int(name[1]), int(name[2])
-        if s == 0:
-            if p in (1, 2):
-                first_forward(p).start()
-            for copy in second_copies(p):
-                copy.start()
-        elif s in (1, 2):
-            second_forward(p, s).start()
-
-    landed(0)
-    landed(1)
+                here = unit(op).at[part]
+                pltpu.make_async_copy(here, here, recv_sem(op, part)).wait()
+            share(op).start()
+
     mine = PLACE["o00"]
-    for i in range(BLOCKS):
-        kv[mine, 0, i] = k_in[placed[i]]
-        kv[mine, 1, i] = v_in[placed[i]]
-    for copy in first_copies():
-        copy.start()
+    for part, source in ((0, k_in), (1, v_in)):
+        landed(part)
+        for i in range(BLOCKS):
+            kv[mine, part, i] = source[placed[i]]
+        begin(first_copies(part))
     share("o00").start()
-    for copy in second_copies(0):
-        copy.start()
 
     landed(2)
     for i in range(BLOCKS):
@@ -227,44 +263,56 @@
     accum[...] = jnp.zeros_like(accum)
     top[...] = jnp.full_like(top, -1e30)
 
-    def step(g, carry):
-        for number, names in enumerate(STEPS):
-            @pl.when(g == number)
-            def _(names=names):
-                for name in names:
-                    if name[0] == "o":
-                        take(name)
-                for name in names:
-                    if name[0] == "s":
-                        take(name)
-
-        for j in range(BLOCKS):
-            keys = jnp.concatenate([kv[g * HALVES + c, 0, j] for c in range(HALVES)], axis=0)
-            scores[j, j * WIDE:QROWS] = lax.dot_general(
-                q_two[j * WIDE:QROWS], jnp.concatenate([keys, keys], axis=1), NT,
-                preferred_element_type=jnp.float32,
-            )
+    plans = plan()
+
+    def events(number):
+        for op in plans[number]:
+            act(op)
+        if number == FETCH_STEP:
+            for fetch in fetches:
+                fetch.start()
+
+    def scored(g, held, j):
+        keys = jnp.concatenate([kv[g * HALVES + c, 0, j] for c in range(HALVES)], axis=0)
+        scores[held, j, j * WIDE:QROWS] = lax.dot_general(
+            q_two[j * WIDE:QROWS], jnp.concatenate([keys, keys], axis=1), NT,
+            preferred_element_type=jnp.float32,
+        )
+
+    def weighed(g, held, i):
+        rows = slice(i * WIDE, (i + 1) * WIDE)
+        old = top[rows]
+        most = old
+        for j in range(i + 1):
+            for t in range(HALVES):
+                most = jnp.maximum(most, scores[held, j, rows, t * HEAD:(t + 1) * HEAD])
+        new = jnp.broadcast_to(jnp.max(most, axis=1, keepdims=True), old.shape)
+        top[rows] = new
+        fade = jnp.exp2(old - new)
+        total = accum[i] * jnp.concatenate([fade, fade], axis=1)
+        shift = jnp.concatenate([new] * HALVES, axis=1)
+        for j in range(i + 1):
+            weights = jnp.exp2(scores[held, j, rows] - shift).astype(jnp.bfloat16)
+            vals = jnp.concatenate([kv[g * HALVES + c, 1, j] for c in range(HALVES)], axis=0)
+            vals = jnp.concatenate([vals, jnp.ones_like(vals)], axis=1)
+            total = total + jnp.dot(weights, vals, preferred_element_type=jnp.float32)
+        accum[i] = total
+
+    def pair(g, held):
         for i in range(BLOCKS):
-            rows = slice(i * WIDE, (i + 1) * WIDE)
-            old = top[rows]
-            most = old
-            for j in range(i + 1):
-                for t in range(HALVES):
-                    most = jnp.maximum(most, scores[j, rows, t * HEAD:(t + 1) * HEAD])
-            new = jnp.broadcast_to(jnp.max(most, axis=1, keepdims=True), old.shape)
-            top[rows] = new
-            fade = jnp.exp2(old - new)
-            total = accum[i] * jnp.concatenate([fade, fade], axis=1)
-            shift = jnp.concatenate([new] * HALVES, axis=1)
-            for j in range(i + 1):
-                weights = jnp.exp2(scores[j, rows] - shift).astype(jnp.bfloat16)
-                vals = jnp.concatenate([kv[g * HALVES + c, 1, j] for c in range(HALVES)], axis=0)
-                vals = jnp.concatenate([vals, jnp.ones_like(vals)], axis=1)
-                total = total + jnp.dot(weights, vals, preferred_element_type=jnp.float32)
-            accum[i] = total
-        return carry
-
-    lax.fori_loop(0, len(STEPS), step, 0)
+            scored(g + 1, 1 - held, i)
+            weighed(g, held, i)
+
+    last = len(STEPS) - 1
+    events(0)
+    for i in range(BLOCKS):
+        scored(0, 0, i)
+
+    for g in range(last):
+        events(g + 1)
+        pair(g, g % 2)
+    for i in range(BLOCKS):
+        weighed(last, last % 2, i)
 
     def give(by, near=False):
         b = lax.rem(st + by, 4)
@@ -293,39 +341,43 @@
         else:
             give(by).start()
 
+    for what in range(3):
+        for by in (1, 2, 3):
+            spread(by, what).wait_send()
+
+        @pl.when(jnp.logical_not(stays))
+        def _(what=what):
+            spread(0, what).wait_send()
+    gone = first_copies(0) + first_copies(1) + first_forwards()
+    for p in range(4):
+        gone += second_copies(p, 0) + second_copies(p, 1) + second_forwards(p)
+        gone += [share("o%d%d" % (p, s)) for s in range(4)]
+    for copy in gone:
+        copy.wait_send()
+
     for fetch in fetches:
         fetch.wait()
-    for h in range(KV_HEADS):
-        pltpu.make_async_copy(o_in.at[h], o_in.at[h], o_recv.at[h]).wait()
-    attended = jnp.concatenate([o_in[h] for h in range(KV_HEADS)], axis=1)
     squares = jnp.zeros((TOKENS, 1), jnp.float32)
     tile = 512
-    for n in range(D // tile):
-        part = jnp.dot(
-            attended, w_v[:, n * tile:(n + 1) * tile], preferred_element_type=jnp.float32
-        )
-        proj[:, n * tile:(n + 1) * tile] = part
-        squares = squares + jnp.sum(part * part, axis=1, keepdims=True)
+    for number, by in enumerate((0, 1, 3, 2)):
+        h = lax.rem(z + by, 4)
+        pltpu.make_async_copy(o_in.at[h], o_in.at[h], o_recv.at[h]).wait()
+        attended = o_in[h]
+        rows = pl.ds(pl.multiple_of(h * WIDE, WIDE), WIDE)
+        for n in range(D // tile):
+            cols = slice(n * tile, (n + 1) * tile)
+            part = jnp.dot(attended, w_v[rows, cols], preferred_element_type=jnp.float32)
+            if number > 0:
+                part = part + proj[:, cols]
+            proj[:, cols] = part
+            if number == 3:
+                squares = squares + jnp.sum(part * part, axis=1, keepdims=True)
     inverse = lax.rsqrt(squares * (1.0 / D) + 1e-06)
     gate = gate_v[pl.ds(noise_ref[0], 1), :] * gain_ref[...]
     out_ref[0] = (
         states_v[0].astype(jnp.float32) + proj[...] * inverse * gate
     ).astype(jnp.bfloat16)
 
-    for what in range(3):
-        for by in (1, 2, 3):
-            spread(by, what).wait_send()
-
-        @pl.when(jnp.logical_not(stays))
-        def _(what=what):
-            spread(0, what).wait_send()
-    for copy in first_copies() + [first_forward(1), first_forward(2)]:
-        copy.wait_send()
-    for p in range(4):
-        for copy in second_copies(p) + [second_forward(p, 1), second_forward(p, 2)]:
-            copy.wait_send()
-        for s in range(4):
-            share("o%d%d" % (p, s)).wait_send()
     for by in (1, 2, 3):
         give(by).wait_send()
 
@@ -353,7 +405,7 @@
             pltpu.VMEM((BLOCKS, TOKENS, HEAD), bf16),
             pltpu.VMEM((QROWS, 2 * HEAD), bf16),
             pltpu.VMEM((32, 2, BLOCKS, TOKENS, HEAD), bf16),
-            pltpu.VMEM((BLOCKS, QROWS, STEP_ROWS), f32),
+            pltpu.VMEM((2, BLOCKS, QROWS, STEP_ROWS), f32),
             pltpu.VMEM((QROWS, HEAD), f32),
             pltpu.VMEM((BLOCKS, WIDE, 2 * HEAD), f32),
             pltpu.VMEM((BLOCKS, TOKENS, WIDE), bf16),
@@ -362,7 +414,7 @@
             pltpu.VMEM((1, TOKENS, D), bf16),
             pltpu.VMEM(gate_table.shape, f32),
             pltpu.VMEM((TOKENS, D), f32),
-            dma((3, 4)), dma((3, 4)), dma((16, 2)), dma((16,)), dma((20,)), dma((16,)),
+            dma((3, 4)), dma((3, 4)), dma((16, 2)), dma((16,)), dma((30,)), dma((16,)),
             dma((4,)), dma((4,)), dma((3,)),
         ],
         compiler_params=pltpu.CompilerParams(

time: 61.9 us -> 58.8 us (0.950)
  Pallas kernels: 59 us -> 55.8 us
    pallas_call x1, Pallas kernels: 59 us -> 55.8 us  [local(): pl.pallas_call(kernel, out_shape=jax.ShapeDtypeStruct((1, TOKENS, D), bf1...]
where the time goes in v2:
time: 58.8 us; the launch traced here: 58.6 us
  Pallas kernels  55.8 us (95%)
  local copies, waits for them, and re-layouts  2.06 us (4%)
  between operations  0.66 us (1%)
    pallas_call x1, Pallas kernels, local(): pl.pallas_call(kernel, out_shape=jax.ShapeDtypeStruct((1, TOKENS, D), bf1...  55.8 us
    unnamed x1, local copies, waits for them, and re-layouts  2.06 us

profile of v2, /device:TPU:1, one launch (start us, length us, event | category | flops | bytes accessed | tf_op | source)
XLA Modules:
  0.0 58.6 jit_solution(14794452056916616449)
XLA Ops:
  0.7 55.8 %attend.1 = bf16[1,128,3072]{2,1,0:T(8,128)(2,1)} custom-call(s32[4]{0:T(128)} %order_ref.1, s32[1]{0:T(128)S(6)} %copy.11.noise_ref, bf16[1,128,1536]{2,1,0:T(8,128)(2,1)} %q_hbm.1, bf16[1,128,512]{2,1,0:T(8,128)(2,1)} %k_hbm.1, bf16[1,128,512]{2,1,0:T(8,128)(2,1)} %v_hbm.1, bf16[1,128,3072]{2,1,0:T(8,128)(2,1)} %states_hbm.1, bf16[1536,3072]{1,0:T(8,128)(2,1)} %w_hbm.1, ...), custom_call_target="tpu_custom_call" | custom-call | flops 9299999744 | bytes 20000000 | tf_op jit(solution)/shard_map/attend/pallas_call | solution.py:397
  56.5 2.1 %copy.12 = bf16[1,128,3072]{2,1,0:T(8,128)(2,1)} copy(bf16[1,128,3072]{2,1,0:T(8,128)(2,1)} %attend.1) | data formatting | bytes 1572864

commit v3 on v2

--- a/solution.py
+++ b/solution.py
@@ -21,40 +21,37 @@
 NT = (((1,), (1,)), ((), ()))
 
 STEPS = (
-    ("o00", "o20"),
-    ("s00", "s10"),
-    ("s20", "o10"),
+    ("o00", "s00"),
+    ("o20", "o10"),
+    ("s10", "s20"),
     ("o02", "o01"),
+    ("s02", "s01"),
     ("o12", "o11"),
-    ("o30", "s01"),
-    ("s11", "s02"),
-    ("o22", "s12"),
-    ("o21", "o03"),
-    ("s30", "s21"),
-    ("o32", "s22"),
-    ("o31", "s03"),
-    ("s31", "o13"),
-    ("o23", "o33"),
-    ("s32", "s23"),
-    ("s33", "s13"),
+    ("o30", "s12"),
+    ("o03", "s11"),
+    ("s30", "o22"),
+    ("s21", "o21"),
+    ("o32", "s03"),
+    ("s31", "o31"),
+    ("o23", "s22"),
+    ("o13", "s32"),
+    ("o33", "s13"),
+    ("s23", "s33"),
 )
 SENDS = {
-    0: ("S00", "S01"),
-    1: ("S11", "S10"),
-    2: ("f3",),
-    3: ("S20", "S21"),
-    4: ("F0",),
+    1: ("o20", "o10", "S10", "S11", "f3"),
+    3: ("o02", "o01", "F0"),
+    4: ("S20", "S21"),
+    5: ("o30",),
     6: ("S31", "S30"),
-    7: ("F2",),
-    8: ("o03", "F1"),
-    10: ("F3",),
-    12: ("o23",),
-    14: ("o33",),
+    8: ("o21", "F2"),
+    9: ("F1",),
+    10: ("o31", "F3"),
 }
 PLACE = {name: i for i, name in enumerate(n for step in STEPS for n in step)}
 HALVES = 2
 STEP_ROWS = HALVES * TOKENS
-FETCH_STEP = 5
+FETCH_STEPS = range(2, 2 + KV_HEADS * GROUP)
 
 
 def unit_number(name):
@@ -88,9 +85,9 @@
 
 def kernel(
     order_ref, noise_ref, q_hbm, k_hbm, v_hbm, states_hbm, w_hbm, gain_ref, gate_hbm,
-    out_ref,
-    q_in, k_in, v_in, q_two, kv, scores, top, accum, o_out, o_in, w_v, states_v, gate_v, proj,
-    qkv_send, qkv_recv, own_recv, sib_recv, own_send, sib_send, o_send, o_recv, fetch_sem,
+    out_hbm,
+    q_in, k_in, v_in, q_two, kv, scores, top, accum, o_out, o_in, w_v, states_v, gate_v, proj, mixed,
+    qkv_send, qkv_recv, own_recv, sib_recv, own_send, sib_send, o_send, o_recv, fetch_sem, out_sem,
 ):
     st = lax.axis_index("stretch")
     mp = lax.axis_index("mp")
@@ -148,11 +145,16 @@
         def _(what=what):
             spread(0, what).start()
 
+    def weights(number):
+        rows = slice(number * TOKENS, (number + 1) * TOKENS)
+        return pltpu.make_async_copy(w_hbm.at[rows], w_v.at[rows], fetch_sem.at[0])
+
     fetches = [
-        pltpu.make_async_copy(w_hbm, w_v, fetch_sem.at[0]),
         pltpu.make_async_copy(gate_hbm, gate_v, fetch_sem.at[1]),
         pltpu.make_async_copy(states_hbm, states_v, fetch_sem.at[2]),
+        pltpu.make_async_copy(w_hbm, w_v, fetch_sem.at[0]),
     ]
+
     def rank_of(b):
         rank, place = jnp.int32(0), order_ref[b]
         for c in range(BLOCKS):
@@ -251,6 +253,7 @@
     share("o00").start()
 
     landed(2)
+    begin(second_copies(0, 0) + second_copies(0, 1))
     for i in range(BLOCKS):
         rows = q_in[placed[i]].astype(jnp.float32) * SCALE
         high = rows.astype(jnp.bfloat16)
@@ -268,9 +271,11 @@
     def events(number):
         for op in plans[number]:
             act(op)
-        if number == FETCH_STEP:
-            for fetch in fetches:
-                fetch.start()
+        if number in FETCH_STEPS:
+            weights(number - FETCH_STEPS[0]).start()
+        if number == FETCH_STEPS[0]:
+            fetches[0].start()
+            fetches[1].start()
 
     def scored(g, held, j):
         keys = jnp.concatenate([kv[g * HALVES + c, 0, j] for c in range(HALVES)], axis=0)
@@ -374,9 +379,17 @@
                 squares = squares + jnp.sum(part * part, axis=1, keepdims=True)
     inverse = lax.rsqrt(squares * (1.0 / D) + 1e-06)
     gate = gate_v[pl.ds(noise_ref[0], 1), :] * gain_ref[...]
-    out_ref[0] = (
-        states_v[0].astype(jnp.float32) + proj[...] * inverse * gate
-    ).astype(jnp.bfloat16)
+
+    def result(n):
+        cols = slice(n * tile, (n + 1) * tile)
+        return pltpu.make_async_copy(mixed.at[:, cols], out_hbm.at[0, :, cols], out_sem.at[n])
+
+    for n in range(D // tile):
+        cols = slice(n * tile, (n + 1) * tile)
+        mixed[:, cols] = (
+            states_v[0, :, cols].astype(jnp.float32) + proj[:, cols] * inverse * gate[:, cols]
+        ).astype(jnp.bfloat16)
+        result(n).start()
 
     for by in (1, 2, 3):
         give(by).wait_send()
@@ -384,6 +397,9 @@
     @pl.when(jnp.logical_not(stays))
     def _():
         give(0).wait_send()
+
+    for n in range(D // tile):
+        result(n).wait()
 
 
 def local(
@@ -398,7 +414,7 @@
         kernel,
         out_shape=jax.ShapeDtypeStruct((1, TOKENS, D), bf16),
         in_specs=[smem, smem, hbm, hbm, hbm, hbm, hbm, vmem, hbm],
-        out_specs=vmem,
+        out_specs=hbm,
         scratch_shapes=[
             pltpu.VMEM((BLOCKS, TOKENS, WIDE), bf16),
             pltpu.VMEM((BLOCKS, TOKENS, HEAD), bf16),
@@ -414,8 +430,9 @@
             pltpu.VMEM((1, TOKENS, D), bf16),
             pltpu.VMEM(gate_table.shape, f32),
             pltpu.VMEM((TOKENS, D), f32),
+            pltpu.VMEM((TOKENS, D), bf16),
             dma((3, 4)), dma((3, 4)), dma((16, 2)), dma((16,)), dma((30,)), dma((16,)),
-            dma((4,)), dma((4,)), dma((3,)),
+            dma((4,)), dma((4,)), dma((3,)), dma((6,)),
         ],
         compiler_params=pltpu.CompilerParams(
             collective_id=0, has_side_effects=True, vmem_limit_bytes=56 * 2**20

time: 58.8 us -> 56.5 us (0.961)
  Pallas kernels: 55.8 us -> 53.5 us
    pallas_call x1, Pallas kernels: 55.8 us -> 53.5 us  [local(): pl.pallas_call(kernel, out_shape=jax.ShapeDtypeStruct((1, TOKENS, D), bf1...]
where the time goes in v3:
time: 56.5 us; the launch traced here: 56.3 us
  Pallas kernels  53.5 us (95%)
  local copies, waits for them, and re-layouts  2.06 us (4%)
  between operations  0.66 us (1%)
    pallas_call x1, Pallas kernels, local(): pl.pallas_call(kernel, out_shape=jax.ShapeDtypeStruct((1, TOKENS, D), bf1...  53.5 us
    unnamed x1, local copies, waits for them, and re-layouts  2.06 us

profile of v3, /device:TPU:1, one launch (start us, length us, event | category | flops | bytes accessed | tf_op | source)
XLA Modules:
  0.0 56.3 jit_solution(15973341276600223042)
XLA Ops:
  0.7 53.5 %attend.1 = bf16[1,128,3072]{2,1,0:T(8,128)(2,1)} custom-call(s32[4]{0:T(128)} %order_ref.1, s32[1]{0:T(128)S(6)} %copy.11.noise_ref, bf16[1,128,1536]{2,1,0:T(8,128)(2,1)} %q_hbm.1, bf16[1,128,512]{2,1,0:T(8,128)(2,1)} %k_hbm.1, bf16[1,128,512]{2,1,0:T(8,128)(2,1)} %v_hbm.1, bf16[1,128,3072]{2,1,0:T(8,128)(2,1)} %states_hbm.1, bf16[1536,3072]{1,0:T(8,128)(2,1)} %w_hbm.1, ...), custom_call_target="tpu_custom_call" | custom-call | flops 9299999744 | bytes 20000000 | tf_op jit(solution)/shard_map/attend/pallas_call | solution.py:413
  54.2 2.1 %copy.12 = bf16[1,128,3072]{2,1,0:T(8,128)(2,1)} copy(bf16[1,128,3072]{2,1,0:T(8,128)(2,1)} %attend.1) | data formatting | bytes 1572864

commit v4 on v3

--- a/solution.py
+++ b/solution.py
@@ -48,6 +48,7 @@
     9: ("F1",),
     10: ("o31", "F3"),
 }
+EARLY = (0, 2)
 PLACE = {name: i for i, name in enumerate(n for step in STEPS for n in step)}
 HALVES = 2
 STEP_ROWS = HALVES * TOKENS
@@ -244,6 +245,9 @@
                 pltpu.make_async_copy(here, here, recv_sem(op, part)).wait()
             share(op).start()
 
+    accum[...] = jnp.zeros_like(accum)
+    top[...] = jnp.full_like(top, -1e30)
+
     mine = PLACE["o00"]
     for part, source in ((0, k_in), (1, v_in)):
         landed(part)
@@ -262,9 +266,6 @@
             at = i * WIDE + g * HEAD
             q_two[at:at + TOKENS, 0:HEAD] = high[:, g * HEAD:(g + 1) * HEAD]
             q_two[at:at + TOKENS, HEAD:2 * HEAD] = low[:, g * HEAD:(g + 1) * HEAD]
-
-    accum[...] = jnp.zeros_like(accum)
-    top[...] = jnp.full_like(top, -1e30)
 
     plans = plan()
 
@@ -314,8 +315,15 @@
         scored(0, 0, i)
 
     for g in range(last):
-        events(g + 1)
-        pair(g, g % 2)
+        if g in EARLY:
+            for i in range(BLOCKS):
+                weighed(g, g % 2, i)
+            events(g + 1)
+            for i in range(BLOCKS):
+                scored(g + 1, 1 - g % 2, i)
+        else:
+            events(g + 1)
+            pair(g, g % 2)
     for i in range(BLOCKS):
         weighed(last, last % 2, i)
 

time: 56.5 us -> 57.4 us (1.016)
  Pallas kernels: 53.5 us -> 54.5 us
    pallas_call x1, Pallas kernels: 53.5 us -> 54.5 us  [local(): pl.pallas_call(kernel, out_shape=jax.ShapeDtypeStruct((1, TOKENS, D), bf1...]
where the time goes in v4:
time: 57.4 us; the launch traced here: 57.2 us
  Pallas kernels  54.5 us (95%)
  local copies, waits for them, and re-layouts  2.06 us (4%)
  between operations  0.66 us (1%)
    pallas_call x1, Pallas kernels, local(): pl.pallas_call(kernel, out_shape=jax.ShapeDtypeStruct((1, TOKENS, D), bf1...  54.5 us
    unnamed x1, local copies, waits for them, and re-layouts  2.06 us

profile of v4, /device:TPU:1, one launch (start us, length us, event | category | flops | bytes accessed | tf_op | source)
XLA Modules:
  0.0 57.2 jit_solution(4791671732999137189)
XLA Ops:
  0.7 54.5 %attend.1 = bf16[1,128,3072]{2,1,0:T(8,128)(2,1)} custom-call(s32[4]{0:T(128)} %order_ref.1, s32[1]{0:T(128)S(6)} %copy.11.noise_ref, bf16[1,128,1536]{2,1,0:T(8,128)(2,1)} %q_hbm.1, bf16[1,128,512]{2,1,0:T(8,128)(2,1)} %k_hbm.1, bf16[1,128,512]{2,1,0:T(8,128)(2,1)} %v_hbm.1, bf16[1,128,3072]{2,1,0:T(8,128)(2,1)} %states_hbm.1, bf16[1536,3072]{1,0:T(8,128)(2,1)} %w_hbm.1, ...), custom_call_target="tpu_custom_call" | custom-call | flops 9299999744 | bytes 20000000 | tf_op jit(solution)/shard_map/attend/pallas_call | solution.py:421
  55.1 2.1 %copy.12 = bf16[1,128,3072]{2,1,0:T(8,128)(2,1)} copy(bf16[1,128,3072]{2,1,0:T(8,128)(2,1)} %attend.1) | data formatting | bytes 1572864
